TPU v7x, 32 devices: a whole 2x2x4 slice. The times are simulated.
32 devices in a mesh: replica: 4 (over y, x), fsdp: 8 (over z, core).
Axes of the slice: x: 2, y: 2, z: 4, core: 2. Of those that a mesh axis runs over, the one named last changes fastest.
Arguments:
- local_weights: bfloat16 [4, 512, 8192], P('replica', 'fsdp'), may hold values from -6 to 6
- base_weights: bfloat16 [512, 8192], P('fsdp'), may hold values from -6 to 6
- momentum: float32 [512, 8192], P('fsdp'), may hold values from -4 to 4
Outputs:
- fragment: bfloat16 [512, 8192], replicated
- new_momentum: float32 [512, 8192], P('fsdp')
All inputs are finite; a program needn't handle non-finite values.
Results may differ from a plain program's by a relative error of at most 0.0053.
Values may be sent and summed in bfloat16 or wider, within the bound.
A program may use at most 128 MiB of HBM per device.

v0:
```python
import jax
import jax.numpy as jnp
from jax import lax
from jax.sharding import PartitionSpec as P

block_width = 128


def quantize(base_weights, local_rows):
    delta = base_weights.astype(jnp.float32) - local_rows.astype(jnp.float32)
    blocks = delta.reshape(delta.shape[0], delta.shape[1] // block_width, block_width)
    largest = jnp.max(jnp.abs(blocks), axis=-1)
    scale = (largest / 448.0 + 1e-06).astype(jnp.bfloat16)
    scale_wide = lax.optimization_barrier(scale).astype(jnp.float32)
    codes = (blocks / scale_wide[..., None]).astype(jnp.bfloat16)
    return (codes, scale)


def dequantize(codes, scale):
    codes_wide = lax.optimization_barrier(codes).astype(jnp.float32)
    scale_wide = lax.optimization_barrier(scale).astype(jnp.float32)
    values = codes_wide * scale_wide[..., None]
    return values.reshape(values.shape[0], values.shape[1] * values.shape[2])


def outer_step(base_rows, momentum_rows, total, groups):
    pseudo = total / groups
    moved = 0.9 * momentum_rows + pseudo
    weights = (base_rows.astype(jnp.float32) - 0.7 * (pseudo + 0.9 * moved)).astype(jnp.bfloat16)
    return (weights, moved)


def local(local_weights, base_weights, momentum):
    groups = lax.axis_size("replica")
    codes, scale = quantize(base_weights, local_weights[0])
    total = lax.psum(dequantize(codes, scale), "replica")
    weights, moved = outer_step(base_weights, momentum, total, groups)
    fragment = lax.all_gather(weights, "fsdp", axis=0, tiled=True)
    return (fragment, moved)


def solution(mesh):
    return jax.shard_map(
        local,
        mesh=mesh,
        in_specs=(P("replica", "fsdp", None), P("fsdp", None), P("fsdp", None)),
        out_specs=(P(), P("fsdp", None)),
        check_vma=False,
    )
```

profile of v0, /device:TPU:0, one launch (start us, length us, event | category | flops | bytes accessed | tf_op | source)
XLA Modules:
  0.0 187.2 jit_solution(1304725811544938985)
XLA Ops:
  7.2 0.0 all-reduce.2.cloned.1.call-start
  7.2 1.7 fusion
  9.0 0.4 copy.5
  9.3 0.6 abs_reduce_fusion
  10.0 0.9 divide_convert_fusion
  10.9 0.6 convert_multiply_fusion
  11.5 0.0 copy-start.1
  11.5 2.5 %copy.8 = f32[8,8,64,128]{3,1,2,0:T(8,128)} copy(f32[8,8,64,128]{3,2,1,0:T(8,128)S(1)} %bitcast.13) | data formatting | bytes 4194304
  14.0 0.0 copy-start
  14.0 0.0 all-reduce.2.cloned.1.call-update
  14.1 0.0 all-gather.2.cloned.1.call-start
  14.1 72.4 %all-reduce.2.cloned.1.call-done = f32[64,8192]{1,0:T(8,128)} async-done(((f32[64,8192]{1,0:T(8,128)}), f32[64,8192]{1,0:T(8,128)}) %all-reduce.2.cloned.1.call-update) | async-done | bytes 2097168 | tf_op jit(solution)/shard_map/psum | solution.py:36
  86.5 0.0 copy-done.1
  86.5 0.0 copy-done
  86.5 3.8 %fusion.1 = (bf16[64,8192]{1,0:T(8,128)(2,1)}, f32[64,8192]{1,0:T(8,128)}) fusion(bf16[64,8192]{1,0:T(8,128)(2,1)S(1)} %copy-done, f32[64,8192]{1,0:T(8,128)} %all-reduce.2.cloned.1.call-done, f32[64,8192]{1,0:T(8,128)S(1)} %copy-done.1), kind=kLoop, calls=%fused_computation.3 | loop fusion | flops 4718592 | bytes 8388608 | tf_op jit(solution)/shard_map/convert_element_type | solution.py:29
  90.4 0.0 all-gather.2.cloned.1.call-update
  90.4 82.2 %all-gather.2.cloned.1.call-done = bf16[512,8192]{1,0:T(8,128)(2,1)} async-done(((bf16[64,8192]{1,0:T(8,128)(2,1)}), bf16[512,8192]{1,0:T(8,128)(2,1)}) %all-gather.2.cloned.1.call-update) | async-done | bytes 8388624 | tf_op jit(solution)/shard_map/all_gather | solution.py:38
  172.6 7.8 %copy.11 = bf16[512,8192]{1,0:T(8,128)(2,1)} copy(bf16[512,8192]{1,0:T(8,128)(2,1)} %all-gather.2.cloned.1.call-done) | data formatting | bytes 16777216
  (2 shorter events, 0.0 us)
Async XLA Ops:
  7.2 79.4 %all-reduce.2.cloned.1.call-start = ((), (), s32[]{:S(2)}) async-start(), calls=%async_computation | async-start | bytes 4194304 | tf_op jit(solution)/shard_map/psum | solution.py:36
  11.5 75.1 %copy-start.1 = (f32[64,8192]{1,0:T(8,128)S(1)}, f32[64,8192]{1,0:T(8,128)}, u32[]{:S(2)}) copy-start(f32[64,8192]{1,0:T(8,128)} %param.5) | copy-start | bytes 6291460
  14.0 72.5 %copy-start = (bf16[64,8192]{1,0:T(8,128)(2,1)S(1)}, bf16[64,8192]{1,0:T(8,128)(2,1)}, u32[]{:S(2)}) copy-start(bf16[64,8192]{1,0:T(8,128)(2,1)} %param.4) | copy-start | bytes 3145732
  14.1 158.6 %all-gather.2.cloned.1.call-start = ((), (), s32[]{:S(2)}) async-start(), calls=%async_computation.1 | async-start | bytes 9437184 | tf_op jit(solution)/shard_map/all_gather | solution.py:38
Sparse Core Ops, SparseCore 0:
  14.2 72.3 all-reduce.1
  90.5 82.0 all-gather.1
where the time goes:
time: 187 us
  waiting for transfers between devices  155 us (83%)
  between operations  14.1 us (8%)
  local copies, waits for them, and re-layouts  10.7 us (6%)
  other arithmetic  7.7 us (4%)
    all_gather x1, waiting for transfers between devices, local(): fragment = lax.all_gather(weights, 'fsdp', axis=0, tiled=True)  82.2 us
    psum x1, waiting for transfers between devices, local(): total = lax.psum(dequantize(codes, scale), 'replica')  72.4 us
    unnamed x7, local copies, waits for them, and re-layouts  10.7 us
    convert_element_type x1, other arithmetic, outer_step(): (base_rows.astype(jnp.float32) - 0.7 * (pseudo + 0.9 * moved)).astype(jnp...  3.83 us
  transfers between devices with their start and end apart: 2, of which 2 were waited for; matrix products, arithmetic and copies ran while one was open for 0% of the time, Pallas kernels for 0%

commit v1 on v0

v1 whole, which is shorter than its diff:
```python
import functools

import jax
import jax.numpy as jnp
from jax import lax
from jax.experimental import pallas as pl
from jax.experimental.pallas import tpu as pltpu
from jax.sharding import PartitionSpec as P

block_width = 128
mesh_ids = pl.DeviceIdType.MESH

chunk_plan = (
    (2, "plane_ba"),
    (1, "plane_ab"),
    (1, "line_ba"),
    (2, "line_ab"),
    (2, "line_ba"),
)
chunk_units = 8


class Slots:
    def __init__(self):
        self.count = 0

    def take(self):
        self.count += 1
        return self.count - 1


def build_kernel(groups, shards, rows, width, chunks):
    outer, inner = 2, groups // 2
    depth = shards // 2
    send_slots, recv_slots = Slots(), Slots()

    def kernel(local_ref, base_ref, momentum_ref, frag_ref, moved_ref, parts, base_own, momentum_own, frag_own, moved_own, send_sem, recv_sem, local_sem):
        send_slots.count = recv_slots.count = 0
        r, f = lax.axis_index("replica"), lax.axis_index("fsdp")
        a, b = r // inner, r % inner
        z, c = f // 2, f % 2
        pending = []

        def device(a_, b_, z_, c_):
            return (a_ * inner + b_, z_ * 2 + c_)

        def send(src, dst, recv_slot, target, when=None):
            copy = pltpu.make_async_remote_copy(
                src_ref=src,
                dst_ref=dst,
                send_sem=send_sem.at[send_slots.take()],
                recv_sem=recv_sem.at[recv_slot],
                device_id=target,
                device_id_type=mesh_ids,
            )
            if when is None:
                copy.start()
            else:
                pl.when(when)(copy.start)
            pending.append((copy, when))

        def arrived(dst, recv_slot):
            pltpu.make_async_remote_copy(
                src_ref=dst,
                dst_ref=dst,
                send_sem=send_sem.at[0],
                recv_sem=recv_sem.at[recv_slot],
                device_id=(r, f),
                device_id_type=mesh_ids,
            ).wait_recv()

        barrier = pltpu.get_barrier_semaphore()
        for step in range(1, groups):
            pl.semaphore_signal(barrier, inc=1, device_id=(lax.rem(r + step, groups), f), device_id_type=mesh_ids)
        pl.semaphore_signal(barrier, inc=1, device_id=device(a, b, z, 1 - c), device_id_type=mesh_ids)

        @pl.when(z > 0)
        def _():
            pl.semaphore_signal(barrier, inc=1, device_id=device(a, b, z - 1, c), device_id_type=mesh_ids)

        @pl.when(z < depth - 1)
        def _():
            pl.semaphore_signal(barrier, inc=1, device_id=device(a, b, z + 1, c), device_id_type=mesh_ids)

        def columns(chunk, owner):
            start, size, _ = chunks[chunk]
            own = size // groups
            return pl.ds(pl.multiple_of(start + owner * own, 128), own)

        def own_columns(chunk):
            start, size, _ = chunks[chunk]
            return pl.ds(start // groups, size // groups)

        def local_copies(chunk):
            here, there = columns(chunk, r), own_columns(chunk)
            return (
                pltpu.make_async_copy(local_ref.at[0, :, here], parts.at[0, :, there], local_sem.at[chunk, 0]),
                pltpu.make_async_copy(base_ref.at[:, here], base_own.at[:, there], local_sem.at[chunk, 1]),
                pltpu.make_async_copy(momentum_ref.at[:, here], momentum_own.at[:, there], local_sem.at[chunk, 2]),
            )

        def result_copies(chunk):
            here, there = columns(chunk, r), own_columns(chunk)
            return (
                pltpu.make_async_copy(frag_own.at[:, there], frag_ref.at[z, c, :, here], local_sem.at[chunk, 3]),
                pltpu.make_async_copy(moved_own.at[:, there], moved_ref.at[:, here], local_sem.at[chunk, 4]),
            )

        for chunk in range(len(chunks)):
            for copy in local_copies(chunk):
                copy.start()
        pl.semaphore_wait(barrier, groups + jnp.where(z > 0, 1, 0) + jnp.where(z < depth - 1, 1, 0))

        scatter_slots = {}
        for chunk in range(len(chunks)):
            for step in range(1, groups):
                slot = scatter_slots[chunk, step] = recv_slots.take()
                owner = lax.rem(r + step, groups)
                send(local_ref.at[0, :, columns(chunk, owner)], parts.at[step, :, own_columns(chunk)], slot, (owner, f))

        def compute(chunk):
            for copy in local_copies(chunk):
                copy.wait()
            for step in range(1, groups):
                arrived(parts.at[step, :, own_columns(chunk)], scatter_slots[chunk, step])
            start, size, _ = chunks[chunk]

            def one_block(index, carry):
                cols = pl.ds(pl.multiple_of(start // groups + index * block_width, block_width), block_width)
                base = base_own[:, cols].astype(jnp.float32)
                total = jnp.zeros((rows, block_width), jnp.float32)
                for step in range(groups):
                    delta = base - parts[step, :, cols].astype(jnp.float32)
                    largest = jnp.max(jnp.abs(delta), axis=-1, keepdims=True)
                    scale = (largest / 448.0 + 1e-06).astype(jnp.bfloat16).astype(jnp.float32)
                    codes = (delta / scale).astype(jnp.bfloat16).astype(jnp.float32)
                    total = total + codes * scale
                pseudo = total / groups
                moved = 0.9 * momentum_own[:, cols] + pseudo
                moved_own[:, cols] = moved.astype(jnp.bfloat16)
                frag_own[:, cols] = (base - 0.7 * (pseudo + 0.9 * moved)).astype(jnp.bfloat16)
                return carry

            lax.fori_loop(0, size // groups // block_width, one_block, 0)
            for copy in result_copies(chunk):
                copy.start()

        def line_slots(length):
            ways = (1,) if length == 2 else (1, -1)
            return {(step, way): recv_slots.take() for step in range(1, length) for way in ways}

        def line_send(slots, step, place, length, neighbour, source, target, when=None):
            for way in (1, -1):
                if length == 2 and way == -1:
                    continue
                if length == 2:
                    send(source(place), target(place), slots[1, 1], neighbour(1 - place), when)
                    continue
                origin = place - way * (step - 1)
                to = place + way
                ok = (origin >= 0) & (origin < length) & (to >= 0) & (to < length)
                if when is not None:
                    ok = ok & when
                send(source(origin), target(origin), slots[step, way], neighbour(to), ok)

        def line_wait(slots, step, place, length, target, when=None):
            for way in (1, -1):
                if length == 2 and way == -1:
                    continue
                if length == 2:
                    origin, ok = 1 - place, when
                else:
                    origin = place - way * step
                    ok = (origin >= 0) & (origin < length)
                    if when is not None:
                        ok = ok & when
                if ok is None:
                    arrived(target(origin), slots[step, way])
                else:
                    pl.when(ok)(functools.partial(arrived, target(origin), slots[step, way]))

        def plane_gather(first, own, target, when=None):
            if first == "b":
                length1, place1, length2, place2 = inner, b, outer, a
                def at(p1, p2):
                    return target(p2, p1)
                def dev(p1, p2):
                    return device(p2, p1, z, c)
            else:
                length1, place1, length2, place2 = outer, a, inner, b
                def at(p1, p2):
                    return target(p1, p2)
                def dev(p1, p2):
                    return device(p1, p2, z, c)
            slots1 = line_slots(length1)
            slots2 = [line_slots(length2) for _ in range(length1)]

            line_send(slots1, 1, place1, length1, lambda p: dev(p, place2), lambda q: own, lambda q: at(q, place2), when)
            line_send(slots2[0], 1, place2, length2, lambda p: dev(place1, p), lambda q: own, lambda q: at(place1, q), when)
            yield
            for step in range(1, length1):
                line_wait(slots1, step, place1, length1, lambda q: at(q, place2), when)
                if step + 1 < length1:
                    line_send(slots1, step + 1, place1, length1, lambda p: dev(p, place2), lambda q: at(q, place2), lambda q: at(q, place2), when)
            for item in range(1, length1):
                p1 = lax.rem(place1 + item, length1)
                line_send(slots2[item], 1, place2, length2, lambda p: dev(place1, p), lambda q: at(p1, q), lambda q: at(p1, q), when)
            yield
            for item in range(length1):
                p1 = lax.rem(place1 + item, length1)
                for step in range(1, length2):
                    line_wait(slots2[item], step, place2, length2, lambda q: at(p1, q), when)
                    if step + 1 < length2:
                        line_send(slots2[item], step + 1, place2, length2, lambda p: dev(place1, p), lambda q: at(p1, q), lambda q: at(p1, q), when)

        def row_block(chunk, z_, c_):
            start, size, _ = chunks[chunk]
            return frag_ref.at[z_, c_, :, pl.ds(start, size)]

        def piece(chunk, z_):
            return lambda a_, b_: frag_ref.at[z_, c, :, columns(chunk, a_ * inner + b_)]

        def sibling_send(chunk, z_, slot, when=None):
            send(row_block(chunk, z_, c), row_block(chunk, z_, c), slot, device(a, b, z, 1 - c), when)

        def plane_first(chunk, first):
            own_source = frag_own.at[:, own_columns(chunk)]
            slots = line_slots(depth)
            sibling = {(0, 1): recv_slots.take()}
            for key in slots:
                sibling[key] = recv_slots.take()
            block = lambda q: row_block(chunk, q, c)
            step_z = lambda p: device(a, b, p, c)
            yield from plane_gather(first, own_source, piece(chunk, z))
            result_copies(chunk)[0].wait()
            line_send(slots, 1, z, depth, step_z, block, block)
            sibling_send(chunk, z, sibling[0, 1])
            yield
            for step in range(1, depth):
                line_wait(slots, step, z, depth, block)
                if step + 1 < depth:
                    line_send(slots, step + 1, z, depth, step_z, block, block)
                for way in (1, -1):
                    q = z - way * step
                    sibling_send(chunk, q, sibling[step, way], (q >= 0) & (q < depth))
                yield
            arrived(row_block(chunk, z, 1 - c), sibling[0, 1])
            for step in range(1, depth):
                for way in (1, -1):
                    q = z - way * step
                    pl.when((q >= 0) & (q < depth))(functools.partial(arrived, row_block(chunk, q, 1 - c), sibling[step, way]))

        def line_first(chunk, first):
            own_source = frag_own.at[:, own_columns(chunk)]
            slots = line_slots(depth)
            sibling = {(0, 1): recv_slots.take()}
            for key in slots:
                sibling[key] = recv_slots.take()
            own_piece = lambda q: piece(chunk, q)(a, b)
            step_z = lambda p: device(a, b, p, c)
            line_send(slots, 1, z, depth, step_z, lambda q: own_source, own_piece)
            gathers = [(plane_gather(first, own_source, piece(chunk, z)), z, (0, 1), None)]
            next(gathers[0][0])
            yield
            for step in range(1, depth):
                line_wait(slots, step, z, depth, own_piece)
                if step + 1 < depth:
                    line_send(slots, step + 1, z, depth, step_z, own_piece, own_piece)
                for way in (1, -1):
                    q = z - way * step
                    ok = (q >= 0) & (q < depth)
                    gather = plane_gather(first, own_piece(q), piece(chunk, q), ok)
                    next(gather)
                    gathers.append((gather, q, (step, way), ok))
                next(gathers[0][0] if step == 1 else gathers[2 * step - 3][0])
                if step > 1:
                    next(gathers[2 * step - 2][0])
                yield
            for gather in gathers[2 * depth - 3:]:
                next(gather[0])
            yield
            for index, (gather, q, key, ok) in enumerate(gathers):
                for _ in gather:
                    pass
                if index == 0:
                    result_copies(chunk)[0].wait()
                sibling_send(chunk, q, sibling[key], ok)
                if index % 2 == 0:
                    yield
            for _, q, key, ok in gathers:
                take = functools.partial(arrived, row_block(chunk, q, 1 - c), sibling[key])
                if ok is None:
                    take()
                else:
                    pl.when(ok)(take)

        def momentum_gather(chunk):
            target = lambda a_, b_: moved_ref.at[:, columns(chunk, a_ * inner + b_)]
            yield from plane_gather("ba"[chunk % 2], moved_own.at[:, own_columns(chunk)], target)
            result_copies(chunk)[1].wait()

        running = []

        def advance():
            for plan in list(running):
                try:
                    next(plan)
                except StopIteration:
                    running.remove(plan)

        later = []
        for chunk, (_, _, plan) in enumerate(chunks):
            compute(chunk)
            gather = plane_first if plan.startswith("plane") else line_first
            new = gather(chunk, plan[-2])
            next(new)
            advance()
            running.append(new)
            later.append(momentum_gather(chunk))
        for plan in later:
            next(plan)
        running.extend(later)
        while running:
            advance()
        for copy, when in pending:
            if when is None:
                copy.wait_send()
            else:
                pl.when(when)(copy.wait_send)

    return kernel, send_slots, recv_slots


def local(groups, shards, local_weights, base_weights, momentum):
    rows, width = base_weights.shape
    chunks, start = [], 0
    for units, plan in chunk_plan:
        size = units * (width // chunk_units)
        chunks.append((start, size, plan))
        start += size
    kernel, send_slots, recv_slots = build_kernel(groups, shards, rows, width, chunks)
    own = width // groups
    depth = shards // 2
    any_spec = pl.BlockSpec(memory_space=pl.ANY)

    def call(sends, receives):
        return pl.pallas_call(
            kernel,
            out_shape=(
                jax.ShapeDtypeStruct((depth, 2, rows, width), jnp.bfloat16),
                jax.ShapeDtypeStruct((rows, width), jnp.bfloat16),
            ),
            in_specs=[any_spec] * 3,
            out_specs=[any_spec] * 2,
            scratch_shapes=[
                pltpu.VMEM((groups, rows, own), jnp.bfloat16),
                pltpu.VMEM((rows, own), jnp.bfloat16),
                pltpu.VMEM((rows, own), jnp.float32),
                pltpu.VMEM((rows, own), jnp.bfloat16),
                pltpu.VMEM((rows, own), jnp.bfloat16),
                pltpu.SemaphoreType.DMA((sends,)),
                pltpu.SemaphoreType.DMA((receives,)),
                pltpu.SemaphoreType.DMA((len(chunks), 5)),
            ],
            compiler_params=pltpu.CompilerParams(collective_id=0, has_side_effects=True, vmem_limit_bytes=24 * 2**20),
        )

    jax.eval_shape(call(1024, 1024), local_weights, base_weights, momentum)
    fragment, moved = call(send_slots.count, recv_slots.count)(local_weights, base_weights, momentum)
    return fragment.reshape(shards * rows, width), moved.astype(jnp.float32)


def solution(mesh):
    return jax.shard_map(
        functools.partial(local, mesh.shape["replica"], mesh.shape["fsdp"]),
        mesh=mesh,
        in_specs=(P("replica", "fsdp", None), P("fsdp", None), P("fsdp", None)),
        out_specs=(P(), P("fsdp", None)),
        check_vma=False,
    )
```

time: 187 us -> 91.7 us (0.49)
  waiting for transfers between devices: 155 us -> 0 us
  Pallas kernels: 0 us -> 74.2 us
  between operations: 14.1 us -> 0.66 us
  other arithmetic: 7.7 us -> 1.46 us
  local copies, waits for them, and re-layouts: 10.7 us -> 15 us
    all_gather x1 -> x0, waiting for transfers between devices: 82.2 us -> none  [local(): fragment = lax.all_gather(weights, 'fsdp', axis=0, tiled=True)]
    pallas_call x0 -> x1, Pallas kernels: none -> 74.2 us  [local(): call(send_slots.count, recv_slots.count)]
    psum x1 -> x0, waiting for transfers between devices: 72.4 us -> none  [local(): total = lax.psum(dequantize(codes, scale), 'replica')]
    unnamed x7 -> x9, local copies, waits for them, and re-layouts: 10.7 us -> 15 us
    convert_element_type x4 -> x1, other arithmetic: 4.73 us -> 1.46 us  [local(): return (fragment.reshape(shards * rows, width), moved.astype(jnp.float32))]
  transfers between devices with their start and end apart: 2 -> 0, of which waited for: 2 -> 0; matrix products, arithmetic and copies ran while one was open for 0% -> 0% of each run, Pallas kernels for 0% -> 0%
where the time goes in v1:
time: 91.7 us; the launch traced here: 91.4 us
  Pallas kernels  74.2 us (81%)
  local copies, waits for them, and re-layouts  15 us (16%)
  other arithmetic  1.46 us (2%)
    pallas_call x1, Pallas kernels, local(): call(send_slots.count, recv_slots.count)  74.2 us
    unnamed x9, local copies, waits for them, and re-layouts  15 us

profile of v1, /device:TPU:0, one launch (start us, length us, event | category | flops | bytes accessed | tf_op | source)
XLA Modules:
  0.0 91.4 jit_solution(8847893248149723025)
XLA Ops:
  0.6 0.0 copy-start.1
  0.6 1.6 %copy-done.1 = f32[64,8192]{1,0:T(8,128)S(1)} copy-done((f32[64,8192]{1,0:T(8,128)S(1)}, f32[64,8192]{1,0:T(8,128)}, u32[]{:S(2)}) %copy-start.1) | copy-done | bytes 2097176
  2.2 0.0 copy-start.2
  2.2 1.2 %copy-done.2 = bf16[1,64,8192]{2,1,0:T(8,128)(2,1)S(1)} copy-done((bf16[1,64,8192]{2,1,0:T(8,128)(2,1)S(1)}, bf16[1,64,8192]{2,1,0:T(8,128)(2,1)}, u32[]{:S(2)}) %copy-start.2) | copy-done | bytes 1048600
  3.4 0.0 copy-start.3
  3.4 1.2 %copy-done.3 = bf16[64,8192]{1,0:T(8,128)(2,1)S(1)} copy-done((bf16[64,8192]{1,0:T(8,128)(2,1)S(1)}, bf16[64,8192]{1,0:T(8,128)(2,1)}, u32[]{:S(2)}) %copy-start.3) | copy-done | bytes 1048600
  4.7 74.2 %shard_map.50 = (bf16[4,2,64,8192]{3,2,1,0:T(8,128)(2,1)S(1)}, bf16[64,8192]{1,0:T(8,128)(2,1)S(1)}) custom-call(bf16[1,64,8192]{2,1,0:T(8,128)(2,1)S(1)} %copy-done.2, bf16[64,8192]{1,0:T(8,128)(2,1)S(1)} %copy-done.3, f32[64,8192]{1,0:T(8,128)S(1)} %copy-done.1), custom_call_target="tpu_custom_call" | custom-call | tf_op jit(solution)/shard_map/pallas_call | solution.py:369
  78.9 0.0 copy-start
  78.9 3.2 %copy-done = bf16[4,2,64,8192]{3,2,1,0:T(8,128)(2,1)} copy-done((bf16[4,2,64,8192]{3,2,1,0:T(8,128)(2,1)}, bf16[4,2,64,8192]{3,2,1,0:T(8,128)(2,1)S(1)}, u32[]{:S(2)}) %copy-start) | copy-done | bytes 8388632
  82.1 1.5 %convert_element_type.3 = f32[64,8192]{1,0:T(8,128)} convert(bf16[64,8192]{1,0:T(8,128)(2,1)S(1)} %get-tuple-element.5) | non-fusion elementwise | flops 524288 | bytes 3145728 | tf_op jit(solution)/shard_map/convert_element_type | solution.py:370
  83.6 7.8 %copy.6 = bf16[512,8192]{1,0:T(8,128)(2,1)} copy(bf16[512,8192]{1,0:T(8,128)(2,1)} %bitcast.1) | data formatting | bytes 16777216
Async XLA Ops:
  0.6 1.6 %copy-start.1 = (f32[64,8192]{1,0:T(8,128)S(1)}, f32[64,8192]{1,0:T(8,128)}, u32[]{:S(2)}) copy-start(f32[64,8192]{1,0:T(8,128)} %momentum_ref.1) | copy-start | bytes 6291460
  2.2 1.2 %copy-start.2 = (bf16[1,64,8192]{2,1,0:T(8,128)(2,1)S(1)}, bf16[1,64,8192]{2,1,0:T(8,128)(2,1)}, u32[]{:S(2)}) copy-start(bf16[1,64,8192]{2,1,0:T(8,128)(2,1)} %local_ref.1) | copy-start | bytes 3145732
  3.4 1.2 %copy-start.3 = (bf16[64,8192]{1,0:T(8,128)(2,1)S(1)}, bf16[64,8192]{1,0:T(8,128)(2,1)}, u32[]{:S(2)}) copy-start(bf16[64,8192]{1,0:T(8,128)(2,1)} %base_ref.1) | copy-start | bytes 3145732
  78.9 3.2 %copy-start = (bf16[4,2,64,8192]{3,2,1,0:T(8,128)(2,1)}, bf16[4,2,64,8192]{3,2,1,0:T(8,128)(2,1)S(1)}, u32[]{:S(2)}) copy-start(bf16[4,2,64,8192]{3,2,1,0:T(8,128)(2,1)S(1)} %get-tuple-element.4) | copy-start | bytes 25165828

commit v2 on v1

--- a/solution.py
+++ b/solution.py
@@ -12,10 +12,8 @@
 
 chunk_plan = (
     (2, "plane_ba"),
-    (1, "plane_ab"),
-    (1, "line_ba"),
-    (2, "line_ab"),
-    (2, "line_ba"),
+    (3, "line_ab"),
+    (3, "line_ba"),
 )
 chunk_units = 8
 
@@ -347,11 +345,11 @@
         return pl.pallas_call(
             kernel,
             out_shape=(
-                jax.ShapeDtypeStruct((depth, 2, rows, width), jnp.bfloat16),
+                pltpu.VMEM((depth, 2, rows, width), jnp.bfloat16),
                 jax.ShapeDtypeStruct((rows, width), jnp.bfloat16),
             ),
             in_specs=[any_spec] * 3,
-            out_specs=[any_spec] * 2,
+            out_specs=[pl.BlockSpec(memory_space=pltpu.VMEM), any_spec],
             scratch_shapes=[
                 pltpu.VMEM((groups, rows, own), jnp.bfloat16),
                 pltpu.VMEM((rows, own), jnp.bfloat16),
@@ -362,7 +360,7 @@
                 pltpu.SemaphoreType.DMA((receives,)),
                 pltpu.SemaphoreType.DMA((len(chunks), 5)),
             ],
-            compiler_params=pltpu.CompilerParams(collective_id=0, has_side_effects=True, vmem_limit_bytes=24 * 2**20),
+            compiler_params=pltpu.CompilerParams(collective_id=0, has_side_effects=True, vmem_limit_bytes=58 * 2**20 - 2 * shards * rows * width),
         )
 
     jax.eval_shape(call(1024, 1024), local_weights, base_weights, momentum)

time: 91.7 us -> 66.1 us (0.72)
  Pallas kernels: 74.2 us -> 60.5 us
  local copies, waits for them, and re-layouts: 15 us -> 3.4 us
    pallas_call x1, Pallas kernels: 74.2 us -> 60.5 us  [local(): call(send_slots.count, recv_slots.count)]
    unnamed x9 -> x3, local copies, waits for them, and re-layouts: 15 us -> 3.4 us
where the time goes in v2:
time: 66.1 us; the launch traced here: 66 us
  Pallas kernels  60.5 us (92%)
  local copies, waits for them, and re-layouts  3.4 us (5%)
  other arithmetic  1.46 us (2%)
    pallas_call x1, Pallas kernels, local(): call(send_slots.count, recv_slots.count)  60.5 us
    unnamed x3, local copies, waits for them, and re-layouts  3.4 us
    convert_element_type x1, other arithmetic, local(): return (fragment.reshape(shards * rows, width), moved.astype(jnp.float32))  1.46 us

profile of v2, /device:TPU:0, one launch (start us, length us, event | category | flops | bytes accessed | tf_op | source)
XLA Modules:
  0.0 66.0 jit_solution(2499300801315364989)
XLA Ops:
  0.6 60.5 %shard_map.50 = (bf16[4,2,64,8192]{3,2,1,0:T(8,128)(2,1)S(1)}, bf16[64,8192]{1,0:T(8,128)(2,1)}) custom-call(bf16[1,64,8192]{2,1,0:T(8,128)(2,1)} %local_ref.1, bf16[64,8192]{1,0:T(8,128)(2,1)} %base_ref.1, f32[64,8192]{1,0:T(8,128)} %momentum_ref.1), custom_call_target="tpu_custom_call" | custom-call | tf_op jit(solution)/shard_map/pallas_call | solution.py:367
  61.1 0.0 copy-start
  61.1 3.4 %copy.6 = bf16[512,8192]{1,0:T(8,128)(2,1)} copy(bf16[512,8192]{1,0:T(8,128)(2,1)S(1)} %bitcast.1) | data formatting | bytes 16777216
  64.5 0.0 copy-done
  64.5 1.5 %convert_element_type.3 = f32[64,8192]{1,0:T(8,128)} convert(bf16[64,8192]{1,0:T(8,128)(2,1)S(1)} %copy-done) | non-fusion elementwise | flops 524288 | bytes 3145728 | tf_op jit(solution)/shard_map/convert_element_type | solution.py:368
Async XLA Ops:
  61.1 3.4 %copy-start = (bf16[64,8192]{1,0:T(8,128)(2,1)S(1)}, bf16[64,8192]{1,0:T(8,128)(2,1)}, u32[]{:S(2)}) copy-start(bf16[64,8192]{1,0:T(8,128)(2,1)} %get-tuple-element.5) | copy-start | bytes 3145732

commit v3 on v2

--- a/solution.py
+++ b/solution.py
@@ -313,7 +313,7 @@
             new = gather(chunk, plan[-2])
             next(new)
             advance()
-            running.append(new)
+            running.insert(0, new)
             later.append(momentum_gather(chunk))
         for plan in later:
             next(plan)

time: 66.1 us -> 63.6 us (0.962)
  Pallas kernels: 60.5 us -> 57.9 us
    pallas_call x1, Pallas kernels: 60.5 us -> 57.9 us  [local(): call(send_slots.count, recv_slots.count)]
where the time goes in v3:
time: 63.6 us; the launch traced here: 63.4 us
  Pallas kernels  57.9 us (91%)
  local copies, waits for them, and re-layouts  3.4 us (5%)
  other arithmetic  1.46 us (2%)
  between operations  0.65 us (1%)
    pallas_call x1, Pallas kernels, local(): call(send_slots.count, recv_slots.count)  57.9 us
    unnamed x3, local copies, waits for them, and re-layouts  3.4 us
    convert_element_type x1, other arithmetic, local(): return (fragment.reshape(shards * rows, width), moved.astype(jnp.float32))  1.46 us

profile of v3, /device:TPU:0, one launch (start us, length us, event | category | flops | bytes accessed | tf_op | source)
XLA Modules:
  0.0 63.4 jit_solution(8949068969581978263)
XLA Ops:
  0.6 57.9 %shard_map.50 = (bf16[4,2,64,8192]{3,2,1,0:T(8,128)(2,1)S(1)}, bf16[64,8192]{1,0:T(8,128)(2,1)}) custom-call(bf16[1,64,8192]{2,1,0:T(8,128)(2,1)} %local_ref.1, bf16[64,8192]{1,0:T(8,128)(2,1)} %base_ref.1, f32[64,8192]{1,0:T(8,128)} %momentum_ref.1), custom_call_target="tpu_custom_call" | custom-call | tf_op jit(solution)/shard_map/pallas_call | solution.py:367
  58.6 0.0 copy-start
  58.6 3.4 %copy.6 = bf16[512,8192]{1,0:T(8,128)(2,1)} copy(bf16[512,8192]{1,0:T(8,128)(2,1)S(1)} %bitcast.1) | data formatting | bytes 16777216
  62.0 0.0 copy-done
  62.0 1.5 %convert_element_type.3 = f32[64,8192]{1,0:T(8,128)} convert(bf16[64,8192]{1,0:T(8,128)(2,1)S(1)} %copy-done) | non-fusion elementwise | flops 524288 | bytes 3145728 | tf_op jit(solution)/shard_map/convert_element_type | solution.py:368
Async XLA Ops:
  58.6 3.4 %copy-start = (bf16[64,8192]{1,0:T(8,128)(2,1)S(1)}, bf16[64,8192]{1,0:T(8,128)(2,1)}, u32[]{:S(2)}) copy-start(bf16[64,8192]{1,0:T(8,128)(2,1)} %get-tuple-element.5) | copy-start | bytes 3145732

commit v4 on v3

--- a/solution.py
+++ b/solution.py
@@ -276,7 +276,6 @@
                 yield
             for gather in gathers[2 * depth - 3:]:
                 next(gather[0])
-            yield
             for index, (gather, q, key, ok) in enumerate(gathers):
                 for _ in gather:
                     pass

time: 63.6 us -> 62.9 us (0.989)
  Pallas kernels: 57.9 us -> 57.2 us
    pallas_call x1, Pallas kernels: 57.9 us -> 57.2 us  [local(): call(send_slots.count, recv_slots.count)]
where the time goes in v4:
time: 62.9 us; the launch traced here: 62.7 us
  Pallas kernels  57.2 us (91%)
  local copies, waits for them, and re-layouts  3.4 us (5%)
  other arithmetic  1.46 us (2%)
  between operations  0.65 us (1%)
    pallas_call x1, Pallas kernels, local(): call(send_slots.count, recv_slots.count)  57.2 us
    unnamed x3, local copies, waits for them, and re-layouts  3.4 us
    convert_element_type x1, other arithmetic, local(): return (fragment.reshape(shards * rows, width), moved.astype(jnp.float32))  1.46 us

profile of v4, /device:TPU:0, one launch (start us, length us, event | category | flops | bytes accessed | tf_op | source)
XLA Modules:
  0.0 62.7 jit_solution(10293979812418026083)
XLA Ops:
  0.6 57.2 %shard_map.50 = (bf16[4,2,64,8192]{3,2,1,0:T(8,128)(2,1)S(1)}, bf16[64,8192]{1,0:T(8,128)(2,1)}) custom-call(bf16[1,64,8192]{2,1,0:T(8,128)(2,1)} %local_ref.1, bf16[64,8192]{1,0:T(8,128)(2,1)} %base_ref.1, f32[64,8192]{1,0:T(8,128)} %momentum_ref.1), custom_call_target="tpu_custom_call" | custom-call | tf_op jit(solution)/shard_map/pallas_call | solution.py:366
  57.9 0.0 copy-start
  57.9 3.4 %copy.6 = bf16[512,8192]{1,0:T(8,128)(2,1)} copy(bf16[512,8192]{1,0:T(8,128)(2,1)S(1)} %bitcast.1) | data formatting | bytes 16777216
  61.3 0.0 copy-done
  61.3 1.5 %convert_element_type.3 = f32[64,8192]{1,0:T(8,128)} convert(bf16[64,8192]{1,0:T(8,128)(2,1)S(1)} %copy-done) | non-fusion elementwise | flops 524288 | bytes 3145728 | tf_op jit(solution)/shard_map/convert_element_type | solution.py:367
Async XLA Ops:
  57.9 3.4 %copy-start = (bf16[64,8192]{1,0:T(8,128)(2,1)S(1)}, bf16[64,8192]{1,0:T(8,128)(2,1)}, u32[]{:S(2)}) copy-start(bf16[64,8192]{1,0:T(8,128)(2,1)} %get-tuple-element.5) | copy-start | bytes 3145732
